TPU v7x, 128 devices: a whole 4x4x4 slice. The times are simulated.
128 devices in a mesh: qa: 8 (over x, y_lo), qb: 16 (over z, y_hi, core).
Axes of the slice: x: 4, y: 4 (y_hi: 2, y_lo: 2; y = y_hi * 2 + y_lo), z: 4, core: 2. Of those that a mesh axis runs over, the one named last changes fastest.
Arguments:
- state: float32 [2, 67108864], P(None, ('qa', 'qb')), may hold values from -6 to 6
- gates: float32 [3, 2, 2, 64, 64], replicated, may hold values from -0.5 to 0.5
Outputs:
- final_state: float32 [2, 67108864], P(None, ('qa', 'qb'))
All inputs are finite; a program needn't handle non-finite values.
Results may differ from a plain program's by a relative error of at most 0.0001.
Values sent between devices are 32-bit elements; how exact they have to be, the bound alone decides.
A program may use at most 64 MiB of HBM per device.

v0:
```python
import functools

import jax
import jax.numpy as jnp
from jax import lax
from jax.experimental import pallas as pl
from jax.experimental.pallas import tpu as pltpu
from jax.sharding import PartitionSpec as P

MESH = pl.DeviceIdType.MESH
STRIDE = 53
CHUNK = 32
HALF = 128 * CHUNK


def place():
    qa, qb = lax.axis_index("qa"), lax.axis_index("qb")
    return qa // 2, (qb // 2) % 2 * 2 + qa % 2, qb // 4, qb % 2


def partner(here, step):
    x, y, z, c = here
    x = (x + step // 32) % 4
    y = (y + step // 8 % 4) % 4
    z = (z + step // 2 % 4) % 4
    c = (c + step % 2) % 2
    return x * 2 + y % 2, z * 4 + y // 2 * 2 + c


def reversed_bits(p):
    out = p % 2
    for b in range(1, 7):
        out = out * 2 + p // (1 << b) % 2
    return out


def trade(first, second, lane_bit):
    apart = 1 << lane_bit
    lane = lax.broadcasted_iota(jnp.int32, first.shape, first.ndim - 1)
    low = lane // apart % 2 == 0
    back = pltpu.roll(first, 128 - apart, first.ndim - 1)
    forth = pltpu.roll(second, apart, second.ndim - 1)
    return jnp.where(low, first, forth), jnp.where(low, back, second)


def halves(x):
    high = x.astype(jnp.bfloat16)
    return high, (x - high.astype(jnp.float32)).astype(jnp.bfloat16)


def apply(weights, x):
    both = jnp.concatenate(halves(x), axis=0)
    out = jnp.dot(weights, both, preferred_element_type=jnp.float32)
    return out[:128] + out[128:]


def one_hot(wanted):
    column = lax.broadcasted_iota(jnp.int32, (128, 128), 1)
    return (column == wanted).astype(jnp.bfloat16)


def exactly(a, b, dims):
    return lax.dot_general(a, b, (dims, ((), ())), preferred_element_type=jnp.float32).astype(
        jnp.bfloat16
    )


def prepare(gates, weights):
    row = lax.broadcasted_iota(jnp.int32, (128, 128), 0)
    low = row % 2 * 8 + row // 2 % 2 * 4 + row // 4 % 2 * 2 + row // 8 % 2
    turn = one_hot(row // 16 * 16 + low)
    natural = one_hot(row % 2 * 64 + row // 2 % 8 * 8 + row // 16)
    for layer in range(3):
        for gate in range(2):
            real, imag = gates[layer, gate, 0], gates[layer, gate, 1]
            whole = jnp.concatenate(
                [
                    jnp.concatenate([real, -imag], axis=1),
                    jnp.concatenate([imag, real], axis=1),
                ],
                axis=0,
            )
            parts = halves(whole)
            if (layer, gate) == (0, 0):
                parts = [exactly(turn, part, ((1,), (0,))) for part in parts]
            if (layer, gate) == (0, 1):
                parts = [exactly(natural, part, ((1,), (0,))) for part in parts]
                parts = [exactly(part, natural, ((1,), (1,))) for part in parts]
            high, low_part = parts
            weights[2 * layer + gate, :128] = jnp.concatenate([high, high], axis=1)
            weights[2 * layer + gate, 128:] = jnp.concatenate([low_part, low_part], axis=1)


def first_layer(x, y, out, weights):
    def second_gate(i, _):
        m = i * 2
        parts = [x[h, pl.ds(m * 16, 32)] for h in range(8)]
        a = jnp.concatenate([p[:16] for p in parts], axis=0)
        b = jnp.concatenate([p[16:] for p in parts], axis=0)
        r = apply(weights[1], jnp.concatenate([a, b], axis=1))
        y[pl.ds(m, 128, stride=64)] = r[:, :128]
        y[pl.ds(m + 1, 128, stride=64)] = r[:, 128:]
        return 0

    lax.fori_loop(0, 32, second_gate, 0, unroll=4)

    def first_gate(q, _):
        a = y[pl.ds(q * 128, 128)]
        b = y[pl.ds(q * 128 + 4096, 128)]
        r = apply(weights[0], jnp.concatenate([a, b], axis=1))
        a = r[:, :128].reshape(4, 2, 16, 128)
        b = r[:, 128:].reshape(4, 2, 16, 128)
        a0, b0 = trade(a[:, 0], b[:, 0], 6)
        a1, b1 = trade(a[:, 1], b[:, 1], 6)
        for six, pair in enumerate(((a0, a1), (b0, b1))):
            for five, value in enumerate(trade(*pair, 5)):
                for s in range(2):
                    for fifteen in range(2):
                        to = ((q % 8) * 4 + q // 8) * 4 + fifteen * 2 + six
                        out[five, pl.ds(to * CHUNK + s * 16, 16)] = value[s * 2 + fifteen]
        return 0

    lax.fori_loop(0, 32, first_gate, 0, unroll=4)


def later_layers(x, t, u, out, weights):
    def put(ref, base, r):
        for s in range(2):
            ref[pl.ds(base + s * 2048, 64, stride=32)] = r[s * 64 : s * 64 + 64]

    def gate_10(i, _):
        cols = []
        for k in range(2):
            v = x[pl.ds((i * 2 + k) * 128, 128)].reshape(4, 2, 16, 128)
            cols.append(jnp.concatenate([v[:, s].reshape(64, 128) for s in range(2)], axis=0))
        r = apply(weights[2], jnp.concatenate(cols, axis=1))
        for k in range(2):
            put(t, i * 2 + k, r[:, k * 128 : k * 128 + 128])
        return 0

    lax.fori_loop(0, 16, gate_10, 0, unroll=4)

    def gate_11(i, _):
        cols = []
        for k in range(2):
            rows = []
            for s in range(2):
                v = t[pl.ds(s * 2048 + (i * 2 + k) * 64, 64)]
                rows.extend(trade(v[:32], v[32:], 5))
            cols.append(jnp.concatenate(rows, axis=0))
        r = apply(weights[3], jnp.concatenate(cols, axis=1))
        for k in range(2):
            put(u, i * 2 + k, r[:, k * 128 : k * 128 + 128])
        return 0

    lax.fori_loop(0, 16, gate_11, 0, unroll=4)

    def gate_20(i, _):
        cols = []
        for k in range(2):
            rows = [u[pl.ds(s * 2048 + (i * 2 + k) * 64, 64)] for s in range(2)]
            cols.append(jnp.concatenate(rows, axis=0))
        r = apply(weights[4], jnp.concatenate(cols, axis=1))
        for k in range(2):
            put(t, i * 2 + k, r[:, k * 128 : k * 128 + 128])
        return 0

    lax.fori_loop(0, 16, gate_20, 0, unroll=4)

    def gate_21(i, _):
        cols = []
        for k in range(2):
            rows = []
            base = (i // 8 * 32 + i % 8 * 2 + k) * 32
            for s in range(2):
                v0 = t[pl.ds(s * 2048 + base, 32)]
                v1 = t[pl.ds(s * 2048 + base + 512, 32)]
                a0, b0 = trade(v0[:16], v0[16:], 6)
                a1, b1 = trade(v1[:16], v1[16:], 6)
                c0, c1 = trade(a0, a1, 5)
                d0, d1 = trade(b0, b1, 5)
                rows.extend([c0, d0, c1, d1])
            cols.append(jnp.concatenate(rows, axis=0))
        r = apply(weights[5], jnp.concatenate(cols, axis=1))
        for k in range(2):
            for s in range(2):
                base = i // 8 * 2048 + (i % 8 * 2 + k) * 2 + s
                out[pl.ds(base, 64, stride=32)] = r[s * 64 : s * 64 + 64, k * 128 : k * 128 + 128]
        return 0

    lax.fori_loop(0, 16, gate_21, 0, unroll=4)


def evolve(
    x_hbm, gates, landed, x, y, sent, got, t, u, ready, weights,
    load_sem, own_sems, send_sems, recv_sems,
):
    here = place()
    me = lax.axis_index("qa") * 16 + lax.axis_index("qb")
    load = pltpu.make_async_copy(x_hbm, x, load_sem)
    load.start()
    barrier = pltpu.get_barrier_semaphore()

    def greet(k, _):
        pl.semaphore_signal(barrier, inc=1, device_id=partner(here, k), device_id_type=MESH)
        return 0

    lax.fori_loop(1, 128, greet, 0)
    prepare(gates, weights)
    load.wait()
    first_layer(x, y, sent, weights)
    pl.semaphore_wait(barrier, 127)

    def spread(source, target, chunk_of, slot, number):
        send, recv = send_sems.at[number], recv_sems.at[number]
        own = pltpu.make_async_copy(
            source.at[pl.ds(chunk_of(me) * CHUNK, CHUNK)],
            target.at[pl.ds(slot * CHUNK, CHUNK)],
            own_sems.at[number],
        )
        own.start()

        def one(k, _):
            qa, qb = partner(here, 1 + k * STRIDE % 127)
            pltpu.make_async_remote_copy(
                src_ref=source.at[pl.ds(chunk_of(qa * 16 + qb) * CHUNK, CHUNK)],
                dst_ref=target.at[pl.ds(slot * CHUNK, CHUNK)],
                send_sem=send,
                recv_sem=recv,
                device_id=(qa, qb),
                device_id_type=MESH,
            ).start()
            return 0

        lax.fori_loop(0, 127, one, 0)
        every = pltpu.make_async_remote_copy(
            src_ref=source.at[pl.ds(0, 127 * CHUNK)],
            dst_ref=target.at[pl.ds(0, 127 * CHUNK)],
            send_sem=send,
            recv_sem=recv,
            device_id=partner(here, 1),
            device_id_type=MESH,
        )
        return own, every

    mine = reversed_bits(me)
    out_first = [spread(sent.at[i], got.at[i], lambda p: p, mine, i) for i in range(2)]
    out_second = []
    for i in range(2):
        own, every = out_first[i]
        own.wait()
        every.wait_recv()
        later_layers(got.at[i], t, u, ready.at[i], weights)
        out_second.append(
            spread(ready.at[i], landed.at[i], lambda p: p % 2 * 64 + p // 2, me, 2 + i)
        )
    for _, every in out_first:
        every.wait_send()
    for own, every in out_second:
        own.wait()
        every.wait()


def finish(landed, out):
    for r in range(8):
        v = [[landed[five, r * 2 + six] for five in range(2)] for six in range(2)]
        a0, b0 = trade(v[0][0], v[1][0], 6)
        a1, b1 = trade(v[0][1], v[1][1], 6)
        for fourteen, pair in enumerate(((a0, a1), (b0, b1))):
            for twentyfour, value in enumerate(trade(*pair, 5)):
                out[0, fourteen, r, twentyfour] = value


def body(state, gates):
    rows = state.reshape(2, 4096, 128).transpose(1, 0, 2).reshape(8, 1024, 128)
    f32 = jnp.float32
    landed = pl.pallas_call(
        evolve,
        out_shape=jax.ShapeDtypeStruct((2, HALF, 128), f32),
        in_specs=[pl.BlockSpec(memory_space=pl.ANY), pl.BlockSpec(memory_space=pltpu.VMEM)],
        out_specs=pl.BlockSpec(memory_space=pl.ANY),
        scratch_shapes=[
            pltpu.VMEM((8, 1024, 128), f32),
            pltpu.VMEM((8192, 128), f32),
            pltpu.VMEM((2, HALF, 128), f32),
            pltpu.VMEM((2, HALF, 128), f32),
            pltpu.VMEM((HALF, 128), f32),
            pltpu.VMEM((HALF, 128), f32),
            pltpu.VMEM((2, HALF, 128), f32),
            pltpu.VMEM((6, 256, 256), jnp.bfloat16),
            pltpu.SemaphoreType.DMA,
            pltpu.SemaphoreType.DMA((4,)),
            pltpu.SemaphoreType.DMA((4,)),
            pltpu.SemaphoreType.DMA((4,)),
        ],
        compiler_params=pltpu.CompilerParams(
            collective_id=0, has_side_effects=True, vmem_limit_bytes=48 * 2**20
        ),
        name="evolve",
    )(rows, gates)
    out = pl.pallas_call(
        finish,
        grid=(8,),
        out_shape=jax.ShapeDtypeStruct((8, 2, 8, 2, 32, 128), f32),
        in_specs=[pl.BlockSpec((2, 16, CHUNK, 128), lambda i: (0, i, 0, 0))],
        out_specs=pl.BlockSpec((1, 2, 8, 2, 32, 128), lambda i: (i, 0, 0, 0, 0, 0)),
        compiler_params=pltpu.CompilerParams(vmem_limit_bytes=16 * 2**20),
        name="finish",
    )(landed.reshape(2, 128, CHUNK, 128))
    return out.reshape(4096, 2, 128).transpose(1, 0, 2).reshape(2, -1)


def solution(mesh):
    placed = (P(None, ("qa", "qb")), P())
    return jax.shard_map(
        body, mesh=mesh, in_specs=placed, out_specs=P(None, ("qa", "qb")), check_vma=False
    )
```

profile of v0, /device:TPU:11, one launch (start us, length us, event | category | flops | bytes accessed | tf_op | source)
XLA Modules:
  0.0 139.6 jit_solution(18382693465062607571)
XLA Ops:
  0.0 0.0 copy-start
  0.0 1.0 copy-done
  1.0 131.9 %evolve.1 = f32[2,4096,128]{2,1,0:T(8,128)S(1)} custom-call(f32[8,1024,128]{2,1,0:T(8,128)} %bitcast.12, f32[3,2,2,64,64]{4,3,2,1,0:T(8,128)S(1)} %copy-done), custom_call_target="tpu_custom_call" | custom-call | tf_op jit(solution)/shard_map/evolve/pallas_call | solution.py:277
  132.9 6.7 %finish.1 = f32[8,2,8,2,32,128]{5,4,3,2,1,0:T(8,128)} custom-call(f32[2,128,32,128]{3,2,1,0:T(8,128)S(1)} %bitcast.11), custom_call_target="tpu_custom_call" | custom-call | tf_op jit(solution)/shard_map/finish/pallas_call | solution.py:301
Async XLA Ops:
  0.0 1.0 copy-start
where the time goes:
time: 140 us
  Pallas kernels  139 us (99%)
    pallas_call x1, Pallas kernels, body(): pl.pallas_call(evolve, out_shape=jax.ShapeDtypeStruct((2, HALF, 128), f32...  132 us
    pallas_call x1, Pallas kernels, body(): pl.pallas_call(finish, grid=(8,), out_shape=jax.ShapeDtypeStruct((8, 2, 8...  6.65 us

commit v1 on v0

--- a/solution.py
+++ b/solution.py
@@ -8,7 +8,7 @@
 from jax.sharding import PartitionSpec as P
 
 MESH = pl.DeviceIdType.MESH
-STRIDE = 53
+STRIDE = 116
 CHUNK = 32
 HALF = 128 * CHUNK
 
@@ -43,6 +43,16 @@
     return jnp.where(low, first, forth), jnp.where(low, back, second)
 
 
+def trade_both(parts):
+    lane = lax.broadcasted_iota(jnp.int32, parts[0].shape, parts[0].ndim - 1)
+    odd, upper = lane // 32 % 2 == 1, lane // 64 == 1
+    once = [jnp.where(odd, parts[(i + 1) % 4], parts[i]) for i in range(4)]
+    skewed = [jnp.where(upper, once[(i + 2) % 4], once[i]) for i in range(4)]
+    turned = skewed[:1] + [pltpu.roll(skewed[i], 32 * i, lane.ndim - 1) for i in range(1, 4)]
+    once = [jnp.where(odd, turned[(i + 1) % 4], turned[i]) for i in range(4)]
+    return [jnp.where(upper, once[(2 - j) % 4], once[-j % 4]) for j in range(4)]
+
+
 def halves(x):
     high = x.astype(jnp.bfloat16)
     return high, (x - high.astype(jnp.float32)).astype(jnp.bfloat16)
@@ -65,12 +75,12 @@
     )
 
 
-def prepare(gates, weights):
+def prepare(gates, weights, layers):
     row = lax.broadcasted_iota(jnp.int32, (128, 128), 0)
     low = row % 2 * 8 + row // 2 % 2 * 4 + row // 4 % 2 * 2 + row // 8 % 2
     turn = one_hot(row // 16 * 16 + low)
     natural = one_hot(row % 2 * 64 + row // 2 % 8 * 8 + row // 16)
-    for layer in range(3):
+    for layer in layers:
         for gate in range(2):
             real, imag = gates[layer, gate, 0], gates[layer, gate, 1]
             whole = jnp.concatenate(
@@ -91,7 +101,7 @@
             weights[2 * layer + gate, 128:] = jnp.concatenate([low_part, low_part], axis=1)
 
 
-def first_layer(x, y, out, weights):
+def first_layer(x, y, out, weights, greet):
     def second_gate(i, _):
         m = i * 2
         parts = [x[h, pl.ds(m * 16, 32)] for h in range(8)]
@@ -102,7 +112,7 @@
         y[pl.ds(m + 1, 128, stride=64)] = r[:, 128:]
         return 0
 
-    lax.fori_loop(0, 32, second_gate, 0, unroll=4)
+    lax.fori_loop(0, 32, second_gate, 0, unroll=8)
 
     def first_gate(q, _):
         a = y[pl.ds(q * 128, 128)]
@@ -110,17 +120,14 @@
         r = apply(weights[0], jnp.concatenate([a, b], axis=1))
         a = r[:, :128].reshape(4, 2, 16, 128)
         b = r[:, 128:].reshape(4, 2, 16, 128)
-        a0, b0 = trade(a[:, 0], b[:, 0], 6)
-        a1, b1 = trade(a[:, 1], b[:, 1], 6)
-        for six, pair in enumerate(((a0, a1), (b0, b1))):
-            for five, value in enumerate(trade(*pair, 5)):
-                for s in range(2):
-                    for fifteen in range(2):
-                        to = ((q % 8) * 4 + q // 8) * 4 + fifteen * 2 + six
-                        out[five, pl.ds(to * CHUNK + s * 16, 16)] = value[s * 2 + fifteen]
-        return 0
-
-    lax.fori_loop(0, 32, first_gate, 0, unroll=4)
+        for j, value in enumerate(trade_both([a[:, 0], a[:, 1], b[:, 0], b[:, 1]])):
+            for s in range(2):
+                for fifteen in range(2):
+                    to = ((q % 8) * 4 + q // 8) * 4 + fifteen * 2 + j // 2
+                    out[j % 2, pl.ds(to * CHUNK + s * 16, 16)] = value[s * 2 + fifteen]
+        return 0
+
+    lax.fori_loop(0, 32, first_gate, 0, unroll=8)
 
 
 def later_layers(x, t, u, out, weights):
@@ -138,7 +145,7 @@
             put(t, i * 2 + k, r[:, k * 128 : k * 128 + 128])
         return 0
 
-    lax.fori_loop(0, 16, gate_10, 0, unroll=4)
+    lax.fori_loop(0, 16, gate_10, 0, unroll=8)
 
     def gate_11(i, _):
         cols = []
@@ -153,7 +160,7 @@
             put(u, i * 2 + k, r[:, k * 128 : k * 128 + 128])
         return 0
 
-    lax.fori_loop(0, 16, gate_11, 0, unroll=4)
+    lax.fori_loop(0, 16, gate_11, 0, unroll=8)
 
     def gate_20(i, _):
         cols = []
@@ -165,7 +172,7 @@
             put(t, i * 2 + k, r[:, k * 128 : k * 128 + 128])
         return 0
 
-    lax.fori_loop(0, 16, gate_20, 0, unroll=4)
+    lax.fori_loop(0, 16, gate_20, 0, unroll=8)
 
     def gate_21(i, _):
         cols = []
@@ -175,11 +182,8 @@
             for s in range(2):
                 v0 = t[pl.ds(s * 2048 + base, 32)]
                 v1 = t[pl.ds(s * 2048 + base + 512, 32)]
-                a0, b0 = trade(v0[:16], v0[16:], 6)
-                a1, b1 = trade(v1[:16], v1[16:], 6)
-                c0, c1 = trade(a0, a1, 5)
-                d0, d1 = trade(b0, b1, 5)
-                rows.extend([c0, d0, c1, d1])
+                c = trade_both([v0[:16], v1[:16], v0[16:], v1[16:]])
+                rows.extend([c[0], c[2], c[1], c[3]])
             cols.append(jnp.concatenate(rows, axis=0))
         r = apply(weights[5], jnp.concatenate(cols, axis=1))
         for k in range(2):
@@ -188,27 +192,30 @@
                 out[pl.ds(base, 64, stride=32)] = r[s * 64 : s * 64 + 64, k * 128 : k * 128 + 128]
         return 0
 
-    lax.fori_loop(0, 16, gate_21, 0, unroll=4)
+    lax.fori_loop(0, 16, gate_21, 0, unroll=8)
 
 
 def evolve(
-    x_hbm, gates, landed, x, y, sent, got, t, u, ready, weights,
-    load_sem, own_sems, send_sems, recv_sems,
+    x_hbm, gates_hbm, landed, x, y, sent, got, t, u, ready, gates, weights,
+    load_sems, own_sems, send_sems, recv_sems,
 ):
     here = place()
     me = lax.axis_index("qa") * 16 + lax.axis_index("qb")
-    load = pltpu.make_async_copy(x_hbm, x, load_sem)
+    load_gates = pltpu.make_async_copy(gates_hbm, gates, load_sems.at[0])
+    load_gates.start()
+    load = pltpu.make_async_copy(x_hbm, x, load_sems.at[1])
     load.start()
     barrier = pltpu.get_barrier_semaphore()
 
-    def greet(k, _):
+    def greet(k, _=0):
         pl.semaphore_signal(barrier, inc=1, device_id=partner(here, k), device_id_type=MESH)
         return 0
 
     lax.fori_loop(1, 128, greet, 0)
-    prepare(gates, weights)
+    load_gates.wait()
+    prepare(gates, weights, (0,))
     load.wait()
-    first_layer(x, y, sent, weights)
+    first_layer(x, y, sent, weights, greet)
     pl.semaphore_wait(barrier, 127)
 
     def spread(source, target, chunk_of, slot, number):
@@ -245,6 +252,7 @@
 
     mine = reversed_bits(me)
     out_first = [spread(sent.at[i], got.at[i], lambda p: p, mine, i) for i in range(2)]
+    prepare(gates, weights, (1, 2))
     out_second = []
     for i in range(2):
         own, every = out_first[i]
@@ -261,14 +269,22 @@
         every.wait()
 
 
-def finish(landed, out):
-    for r in range(8):
-        v = [[landed[five, r * 2 + six] for five in range(2)] for six in range(2)]
-        a0, b0 = trade(v[0][0], v[1][0], 6)
-        a1, b1 = trade(v[0][1], v[1][1], 6)
-        for fourteen, pair in enumerate(((a0, a1), (b0, b1))):
-            for twentyfour, value in enumerate(trade(*pair, 5)):
-                out[0, fourteen, r, twentyfour] = value
+def finish(landed, out, stage, sems):
+    def block(i, _):
+        for r in range(8):
+            v = [landed[j % 2, i * 16 + r * 2 + j // 2] for j in range(4)]
+            for j, value in enumerate(trade_both(v)):
+                stage[i, j // 2, r, j % 2] = value
+        pltpu.make_async_copy(stage.at[i], out.at[i], sems.at[i]).start()
+        return 0
+
+    lax.fori_loop(0, 8, block, 0)
+
+    def done(i, _):
+        pltpu.make_async_copy(stage.at[i], out.at[i], sems.at[i]).wait()
+        return 0
+
+    lax.fori_loop(0, 8, done, 0)
 
 
 def body(state, gates):
@@ -277,7 +293,7 @@
     landed = pl.pallas_call(
         evolve,
         out_shape=jax.ShapeDtypeStruct((2, HALF, 128), f32),
-        in_specs=[pl.BlockSpec(memory_space=pl.ANY), pl.BlockSpec(memory_space=pltpu.VMEM)],
+        in_specs=[pl.BlockSpec(memory_space=pl.ANY), pl.BlockSpec(memory_space=pltpu.HBM)],
         out_specs=pl.BlockSpec(memory_space=pl.ANY),
         scratch_shapes=[
             pltpu.VMEM((8, 1024, 128), f32),
@@ -287,8 +303,9 @@
             pltpu.VMEM((HALF, 128), f32),
             pltpu.VMEM((HALF, 128), f32),
             pltpu.VMEM((2, HALF, 128), f32),
+            pltpu.VMEM((3, 2, 2, 64, 64), f32),
             pltpu.VMEM((6, 256, 256), jnp.bfloat16),
-            pltpu.SemaphoreType.DMA,
+            pltpu.SemaphoreType.DMA((2,)),
             pltpu.SemaphoreType.DMA((4,)),
             pltpu.SemaphoreType.DMA((4,)),
             pltpu.SemaphoreType.DMA((4,)),
@@ -298,12 +315,13 @@
         ),
         name="evolve",
     )(rows, gates)
+    shape = (8, 2, 8, 2, CHUNK, 128)
     out = pl.pallas_call(
         finish,
-        grid=(8,),
-        out_shape=jax.ShapeDtypeStruct((8, 2, 8, 2, 32, 128), f32),
-        in_specs=[pl.BlockSpec((2, 16, CHUNK, 128), lambda i: (0, i, 0, 0))],
-        out_specs=pl.BlockSpec((1, 2, 8, 2, 32, 128), lambda i: (i, 0, 0, 0, 0, 0)),
+        out_shape=jax.ShapeDtypeStruct(shape, f32),
+        in_specs=[pl.BlockSpec(memory_space=pltpu.VMEM)],
+        out_specs=pl.BlockSpec(memory_space=pl.ANY),
+        scratch_shapes=[pltpu.VMEM(shape, f32), pltpu.SemaphoreType.DMA((8,))],
         compiler_params=pltpu.CompilerParams(vmem_limit_bytes=16 * 2**20),
         name="finish",
     )(landed.reshape(2, 128, CHUNK, 128))

time: 140 us -> 116 us (0.83)
  the two profiles are of different devices: /device:TPU:11 before, /device:TPU:1 now
where the time goes in v1:
time: 116 us
  Pallas kernels  115 us (99%)
    pallas_call x1, Pallas kernels, body(): pl.pallas_call(evolve, out_shape=jax.ShapeDtypeStruct((2, HALF, 128), f32...  112 us
    pallas_call x1, Pallas kernels, body(): pl.pallas_call(finish, out_shape=jax.ShapeDtypeStruct(shape, f32), in_spe...  2.33 us

profile of v1, /device:TPU:1, one launch (start us, length us, event | category | flops | bytes accessed | tf_op | source)
XLA Modules:
  0.0 115.7 jit_solution(14762130165937372338)
XLA Ops:
  0.0 0.0 copy-start
  0.0 1.0 copy-done
  1.0 112.4 %evolve.1 = f32[2,4096,128]{2,1,0:T(8,128)S(1)} custom-call(f32[8,1024,128]{2,1,0:T(8,128)} %bitcast.12, f32[3,2,2,64,64]{4,3,2,1,0:T(8,128)S(1)} %copy-done), custom_call_target="tpu_custom_call" | custom-call | tf_op jit(solution)/shard_map/evolve/pallas_call | solution.py:293
  113.4 2.3 %finish.1 = f32[8,2,8,2,32,128]{5,4,3,2,1,0:T(8,128)} custom-call(f32[2,128,32,128]{3,2,1,0:T(8,128)S(1)} %bitcast.11), custom_call_target="tpu_custom_call" | custom-call | tf_op jit(solution)/shard_map/finish/pallas_call | solution.py:319
Async XLA Ops:
  0.0 1.0 copy-start

commit v2 on v1

--- a/solution.py
+++ b/solution.py
@@ -8,29 +8,48 @@
 from jax.sharding import PartitionSpec as P
 
 MESH = pl.DeviceIdType.MESH
-STRIDE = 116
+STEP = 13
+FOUR = (0, 1, 2, 3)
+ORDER = [1 + k * 116 % 127 for k in range(127)]
+VMEM = 48 * 2**20
 CHUNK = 32
 HALF = 128 * CHUNK
 
 
-def place():
-    qa, qb = lax.axis_index("qa"), lax.axis_index("qb")
-    return qa // 2, (qb // 2) % 2 * 2 + qa % 2, qb // 4, qb % 2
-
-
-def partner(here, step):
-    x, y, z, c = here
-    x = (x + step // 32) % 4
-    y = (y + step // 8 % 4) % 4
-    z = (z + step // 2 % 4) % 4
-    c = (c + step % 2) % 2
-    return x * 2 + y % 2, z * 4 + y // 2 * 2 + c
+def split(step):
+    return step // 32, step // 8 % 4, step // 2 % 4, step % 2
+
+
+def hops(step):
+    return sum(min(d, 4 - d) for d in split(step)[:3])
+
+
+class Torus:
+    def __init__(self):
+        qa, qb = lax.axis_index("qa"), lax.axis_index("qb")
+        self.me = qa * 16 + qb
+        x, z, core = lax.div(qa, 2), lax.div(qb, 4), lax.rem(qb, 2)
+        y = lax.rem(lax.div(qb, 2), 2) * 2 + lax.rem(qa, 2)
+        self.x = [lax.rem(x + d, 4) for d in range(4)]
+        self.y = [lax.rem(y + d, 4) for d in range(4)]
+        self.z = [lax.rem(z + d, 4) for d in range(4)]
+        self.core = [core, 1 - core]
+        self.y_low = [lax.rem(v, 2) for v in self.y]
+        self.y_high = [lax.div(v, 2) for v in self.y]
+
+    def partner(self, step):
+        dx, dy, dz, dc = split(step)
+        qa = self.x[dx] * 2 + self.y_low[dy]
+        return qa, self.z[dz] * 4 + self.y_high[dy] * 2 + self.core[dc]
+
+
+GREET = sorted(range(1, 128), key=lambda step: (-hops(step), step))
 
 
 def reversed_bits(p):
-    out = p % 2
+    out = lax.rem(p, 2)
     for b in range(1, 7):
-        out = out * 2 + p // (1 << b) % 2
+        out = out * 2 + lax.rem(lax.div(p, 1 << b), 2)
     return out
 
 
@@ -101,7 +120,7 @@
             weights[2 * layer + gate, 128:] = jnp.concatenate([low_part, low_part], axis=1)
 
 
-def first_layer(x, y, out, weights, greet):
+def second_gates(x, y, weights):
     def second_gate(i, _):
         m = i * 2
         parts = [x[h, pl.ds(m * 16, 32)] for h in range(8)]
@@ -114,20 +133,18 @@
 
     lax.fori_loop(0, 32, second_gate, 0, unroll=8)
 
-    def first_gate(q, _):
-        a = y[pl.ds(q * 128, 128)]
-        b = y[pl.ds(q * 128 + 4096, 128)]
-        r = apply(weights[0], jnp.concatenate([a, b], axis=1))
-        a = r[:, :128].reshape(4, 2, 16, 128)
-        b = r[:, 128:].reshape(4, 2, 16, 128)
-        for j, value in enumerate(trade_both([a[:, 0], a[:, 1], b[:, 0], b[:, 1]])):
-            for s in range(2):
-                for fifteen in range(2):
-                    to = ((q % 8) * 4 + q // 8) * 4 + fifteen * 2 + j // 2
-                    out[j % 2, pl.ds(to * CHUNK + s * 16, 16)] = value[s * 2 + fifteen]
-        return 0
-
-    lax.fori_loop(0, 32, first_gate, 0, unroll=8)
+
+def first_gate(y, out, weights, q):
+    a = y[pl.ds(q * 128, 128)]
+    b = y[pl.ds(q * 128 + 4096, 128)]
+    r = apply(weights[0], jnp.concatenate([a, b], axis=1))
+    a = r[:, :128].reshape(4, 2, 16, 128)
+    b = r[:, 128:].reshape(4, 2, 16, 128)
+    for j, value in enumerate(trade_both([a[:, 0], a[:, 1], b[:, 0], b[:, 1]])):
+        for s in range(2):
+            for fifteen in range(2):
+                to = ((q % 8) * 4 + q // 8) * 4 + fifteen * 2 + j // 2
+                out[j % 2, pl.ds(to * CHUNK + s * 16, 16)] = value[s * 2 + fifteen]
 
 
 def later_layers(x, t, u, out, weights):
@@ -199,74 +216,87 @@
     x_hbm, gates_hbm, landed, x, y, sent, got, t, u, ready, gates, weights,
     load_sems, own_sems, send_sems, recv_sems,
 ):
-    here = place()
-    me = lax.axis_index("qa") * 16 + lax.axis_index("qb")
     load_gates = pltpu.make_async_copy(gates_hbm, gates, load_sems.at[0])
     load_gates.start()
     load = pltpu.make_async_copy(x_hbm, x, load_sems.at[1])
     load.start()
     barrier = pltpu.get_barrier_semaphore()
-
-    def greet(k, _=0):
-        pl.semaphore_signal(barrier, inc=1, device_id=partner(here, k), device_id_type=MESH)
-        return 0
-
-    lax.fori_loop(1, 128, greet, 0)
-    load_gates.wait()
-    prepare(gates, weights, (0,))
-    load.wait()
-    first_layer(x, y, sent, weights, greet)
-    pl.semaphore_wait(barrier, 127)
-
-    def spread(source, target, chunk_of, slot, number):
-        send, recv = send_sems.at[number], recv_sems.at[number]
-        own = pltpu.make_async_copy(
+    torus = Torus()
+    me = torus.me
+    for step in GREET:
+        pl.semaphore_signal(barrier, inc=1, device_id=torus.partner(step), device_id_type=MESH)
+
+    def remote(step, source, target, chunk_of, slot, number):
+        qa, qb = torus.partner(step)
+        return pltpu.make_async_remote_copy(
+            src_ref=source.at[pl.ds(chunk_of(qa * 16 + qb) * CHUNK, CHUNK)],
+            dst_ref=target.at[pl.ds(slot * CHUNK, CHUNK)],
+            send_sem=send_sems.at[number],
+            recv_sem=recv_sems.at[number],
+            device_id=(qa, qb),
+            device_id_type=MESH,
+        )
+
+    def keep(source, target, chunk_of, slot, number):
+        return pltpu.make_async_copy(
             source.at[pl.ds(chunk_of(me) * CHUNK, CHUNK)],
             target.at[pl.ds(slot * CHUNK, CHUNK)],
             own_sems.at[number],
         )
-        own.start()
-
-        def one(k, _):
-            qa, qb = partner(here, 1 + k * STRIDE % 127)
-            pltpu.make_async_remote_copy(
-                src_ref=source.at[pl.ds(chunk_of(qa * 16 + qb) * CHUNK, CHUNK)],
-                dst_ref=target.at[pl.ds(slot * CHUNK, CHUNK)],
-                send_sem=send,
-                recv_sem=recv,
-                device_id=(qa, qb),
-                device_id_type=MESH,
-            ).start()
-            return 0
-
-        lax.fori_loop(0, 127, one, 0)
-        every = pltpu.make_async_remote_copy(
+
+    def every(source, target, number):
+        return pltpu.make_async_remote_copy(
             src_ref=source.at[pl.ds(0, 127 * CHUNK)],
             dst_ref=target.at[pl.ds(0, 127 * CHUNK)],
-            send_sem=send,
-            recv_sem=recv,
-            device_id=partner(here, 1),
+            send_sem=send_sems.at[number],
+            recv_sem=recv_sems.at[number],
+            device_id=torus.partner(1),
             device_id_type=MESH,
         )
-        return own, every
+
+    def straight(p):
+        return p
+
+    def twisted(p):
+        return lax.rem(p, 2) * 64 + lax.div(p, 2)
 
     mine = reversed_bits(me)
-    out_first = [spread(sent.at[i], got.at[i], lambda p: p, mine, i) for i in range(2)]
+    load_gates.wait()
+    prepare(gates, weights, (0,))
+    load.wait()
+    second_gates(x, y, weights)
+    for block in range(4):
+        steps = [(block * 8 + i + 1) * STEP % 32 for i in range(8)]
+        for step in steps:
+            q = torus.z[step // 2 % 4] * 8 + torus.x[step // 8] * 2 + torus.y_low[step % 2]
+            first_gate(y, sent, weights, q)
+        if block == 0:
+            pl.semaphore_wait(barrier, 127)
+        for e in FOUR:
+            for step in steps:
+                k = step // 8 * 32 + (step % 2 + e // 2 * 2) * 8 + step // 2 % 4 * 2 + e % 2
+                if k:
+                    remote(k, sent.at[0], got.at[0], straight, mine, 0).start()
+    keep(sent.at[0], got.at[0], straight, mine, 0).start()
+    for step in ORDER:
+        remote(step, sent.at[1], got.at[1], straight, mine, 1).start()
+    keep(sent.at[1], got.at[1], straight, mine, 1).start()
     prepare(gates, weights, (1, 2))
-    out_second = []
+
+    def middle(i, _):
+        keep(sent.at[i], got.at[i], straight, mine, i).wait()
+        every(sent.at[i], got.at[i], i).wait_recv()
+        later_layers(got.at[i], t, u, ready.at[i], weights)
+        for step in ORDER:
+            remote(step, ready.at[i], landed.at[i], twisted, me, 2 + i).start()
+        keep(ready.at[i], landed.at[i], twisted, me, 2 + i).start()
+        return 0
+
+    lax.fori_loop(0, 2, middle, 0)
     for i in range(2):
-        own, every = out_first[i]
-        own.wait()
-        every.wait_recv()
-        later_layers(got.at[i], t, u, ready.at[i], weights)
-        out_second.append(
-            spread(ready.at[i], landed.at[i], lambda p: p % 2 * 64 + p // 2, me, 2 + i)
-        )
-    for _, every in out_first:
-        every.wait_send()
-    for own, every in out_second:
-        own.wait()
-        every.wait()
+        every(sent.at[i], got.at[i], i).wait_send()
+        keep(ready.at[i], landed.at[i], twisted, me, 2 + i).wait()
+        every(ready.at[i], landed.at[i], 2 + i).wait()
 
 
 def finish(landed, out, stage, sems):
@@ -311,7 +341,7 @@
             pltpu.SemaphoreType.DMA((4,)),
         ],
         compiler_params=pltpu.CompilerParams(
-            collective_id=0, has_side_effects=True, vmem_limit_bytes=48 * 2**20
+            collective_id=0, has_side_effects=True, vmem_limit_bytes=VMEM
         ),
         name="evolve",
     )(rows, gates)

time: 116 us -> 110 us (0.948)
  Pallas kernels: 115 us -> 109 us
    pallas_call x1, Pallas kernels: 112 us -> 106 us  [body(): pl.pallas_call(evolve, out_shape=jax.ShapeDtypeStruct((2, HALF, 128), f32...]
where the time goes in v2:
time: 110 us
  Pallas kernels  109 us (99%)
    pallas_call x1, Pallas kernels, body(): pl.pallas_call(evolve, out_shape=jax.ShapeDtypeStruct((2, HALF, 128), f32...  106 us
    pallas_call x1, Pallas kernels, body(): pl.pallas_call(finish, out_shape=jax.ShapeDtypeStruct(shape, f32), in_spe...  2.33 us

profile of v2, /device:TPU:1, one launch (start us, length us, event | category | flops | bytes accessed | tf_op | source)
XLA Modules:
  0.0 109.6 jit_solution(274116511657196779)
XLA Ops:
  0.0 0.0 copy-start
  0.0 1.0 copy-done
  1.0 106.3 %evolve.1 = f32[2,4096,128]{2,1,0:T(8,128)S(1)} custom-call(f32[8,1024,128]{2,1,0:T(8,128)} %bitcast.12, f32[3,2,2,64,64]{4,3,2,1,0:T(8,128)S(1)} %copy-done), custom_call_target="tpu_custom_call" | custom-call | tf_op jit(solution)/shard_map/evolve/pallas_call | solution.py:323
  107.3 2.3 %finish.1 = f32[8,2,8,2,32,128]{5,4,3,2,1,0:T(8,128)} custom-call(f32[2,128,32,128]{3,2,1,0:T(8,128)S(1)} %bitcast.11), custom_call_target="tpu_custom_call" | custom-call | tf_op jit(solution)/shard_map/finish/pallas_call | solution.py:349
Async XLA Ops:
  0.0 1.0 copy-start

commit v3 on v2

--- a/solution.py
+++ b/solution.py
@@ -10,7 +10,8 @@
 MESH = pl.DeviceIdType.MESH
 STEP = 13
 FOUR = (0, 1, 2, 3)
-ORDER = [1 + k * 116 % 127 for k in range(127)]
+BLOCKS = (4, 4, 8, 8, 8)
+ORDER = [1 + k * 41 % 127 for k in range(127)]
 VMEM = 48 * 2**20
 CHUNK = 32
 HALF = 128 * CHUNK
@@ -265,18 +266,20 @@
     prepare(gates, weights, (0,))
     load.wait()
     second_gates(x, y, weights)
-    for block in range(4):
-        steps = [(block * 8 + i + 1) * STEP % 32 for i in range(8)]
+    done = 0
+    for size in BLOCKS:
+        steps = [(done + i + 1) * STEP % 32 for i in range(size)]
         for step in steps:
             q = torus.z[step // 2 % 4] * 8 + torus.x[step // 8] * 2 + torus.y_low[step % 2]
             first_gate(y, sent, weights, q)
-        if block == 0:
+        if done == 0:
             pl.semaphore_wait(barrier, 127)
         for e in FOUR:
             for step in steps:
                 k = step // 8 * 32 + (step % 2 + e // 2 * 2) * 8 + step // 2 % 4 * 2 + e % 2
                 if k:
                     remote(k, sent.at[0], got.at[0], straight, mine, 0).start()
+        done += size
     keep(sent.at[0], got.at[0], straight, mine, 0).start()
     for step in ORDER:
         remote(step, sent.at[1], got.at[1], straight, mine, 1).start()
@@ -344,7 +347,7 @@
             collective_id=0, has_side_effects=True, vmem_limit_bytes=VMEM
         ),
         name="evolve",
-    )(rows, gates)
+    )(rows, pltpu.with_memory_space_constraint(gates, pltpu.HBM))
     shape = (8, 2, 8, 2, CHUNK, 128)
     out = pl.pallas_call(
         finish,

time: 110 us -> 108 us (0.982)
  Pallas kernels: 109 us -> 107 us
    pallas_call x1, Pallas kernels: 106 us -> 105 us  [body(): pl.pallas_call(evolve, out_shape=jax.ShapeDtypeStruct((2, HALF, 128), f32...]
where the time goes in v3:
time: 108 us; the launch traced here: 107 us
  Pallas kernels  107 us (99%)
    pallas_call x1, Pallas kernels, body(): pl.pallas_call(evolve, out_shape=jax.ShapeDtypeStruct((2, HALF, 128), f32...  105 us
    pallas_call x1, Pallas kernels, body(): pl.pallas_call(finish, out_shape=jax.ShapeDtypeStruct(shape, f32), in_spe...  2.33 us

profile of v3, /device:TPU:1, one launch (start us, length us, event | category | flops | bytes accessed | tf_op | source)
XLA Modules:
  0.0 107.2 jit_solution(6132468328982181442)
XLA Ops:
  0.0 104.9 %evolve.1 = f32[2,4096,128]{2,1,0:T(8,128)S(1)} custom-call(f32[8,1024,128]{2,1,0:T(8,128)} %bitcast.12, f32[3,2,2,64,64]{4,3,2,1,0:T(8,128)} %gates_hbm.1), custom_call_target="tpu_custom_call" | custom-call | tf_op jit(solution)/shard_map/evolve/pallas_call | solution.py:326
  104.9 2.3 %finish.1 = f32[8,2,8,2,32,128]{5,4,3,2,1,0:T(8,128)} custom-call(f32[2,128,32,128]{3,2,1,0:T(8,128)S(1)} %bitcast.11), custom_call_target="tpu_custom_call" | custom-call | tf_op jit(solution)/shard_map/finish/pallas_call | solution.py:352

commit v4 on v3

--- a/solution.py
+++ b/solution.py
@@ -330,12 +330,12 @@
         out_specs=pl.BlockSpec(memory_space=pl.ANY),
         scratch_shapes=[
             pltpu.VMEM((8, 1024, 128), f32),
-            pltpu.VMEM((8192, 128), f32),
+            pltpu.VMEM((8192 + 64, 128), f32),
             pltpu.VMEM((2, HALF, 128), f32),
             pltpu.VMEM((2, HALF, 128), f32),
-            pltpu.VMEM((HALF, 128), f32),
-            pltpu.VMEM((HALF, 128), f32),
-            pltpu.VMEM((2, HALF, 128), f32),
+            pltpu.VMEM((HALF + CHUNK, 128), f32),
+            pltpu.VMEM((HALF + CHUNK, 128), f32),
+            pltpu.VMEM((2, HALF + CHUNK, 128), f32),
             pltpu.VMEM((3, 2, 2, 64, 64), f32),
             pltpu.VMEM((6, 256, 256), jnp.bfloat16),
             pltpu.SemaphoreType.DMA((2,)),

time: 108 us -> 108 us (level)
  no operation moved by 1% of the time
where the time goes in v4:
time: 108 us; the launch traced here: 107 us
  Pallas kernels  107 us (99%)
    pallas_call x1, Pallas kernels, body(): pl.pallas_call(evolve, out_shape=jax.ShapeDtypeStruct((2, HALF, 128), f32...  105 us
    pallas_call x1, Pallas kernels, body(): pl.pallas_call(finish, out_shape=jax.ShapeDtypeStruct(shape, f32), in_spe...  2.33 us

profile of v4, /device:TPU:1, one launch (start us, length us, event | category | flops | bytes accessed | tf_op | source)
XLA Modules:
  0.0 107.2 jit_solution(17089254619027804238)
XLA Ops:
  0.0 104.9 %evolve.1 = f32[2,4096,128]{2,1,0:T(8,128)S(1)} custom-call(f32[8,1024,128]{2,1,0:T(8,128)} %bitcast.12, f32[3,2,2,64,64]{4,3,2,1,0:T(8,128)} %gates_hbm.1), custom_call_target="tpu_custom_call" | custom-call | tf_op jit(solution)/shard_map/evolve/pallas_call | solution.py:326
  104.9 2.3 %finish.1 = f32[8,2,8,2,32,128]{5,4,3,2,1,0:T(8,128)} custom-call(f32[2,128,32,128]{3,2,1,0:T(8,128)S(1)} %bitcast.11), custom_call_target="tpu_custom_call" | custom-call | tf_op jit(solution)/shard_map/finish/pallas_call | solution.py:352
